TPU v7x, 32 devices: a whole 2x2x4 slice. The times are simulated.
32 devices in a mesh: tm: 4 (over x, core), tile: 8 (over z, y).
Axes of the slice: x: 2, y: 2, z: 4, core: 2. Of those that a mesh axis runs over, the one named last changes fastest.
Arguments:
- advect_east: float32 [4, 2, 96, 1440], P('tm', None, 'tile'), may hold values from -0.15 to 0.15
- advect_north: float32 [4, 2, 96, 1440], P('tm', None, 'tile'), may hold values from -0.15 to 0.15
- diffusion: float32 [4, 2, 96, 1440], P('tm', None, 'tile'), may hold values from 0.06 to 0.22
- background_var: float32 [4, 4, 2, 96, 1440], P('tm', None, None, 'tile'), may hold values from 0.3 to 3
- obs_cell: int32 [4, 8, 256], P('tm', 'tile'), may hold values from 0 to 138239
- obs_value: float32 [4, 8, 256], P('tm', 'tile'), may hold values from -6 to 6
- obs_weight: float32 [4, 8, 256], P('tm', 'tile'), may hold values from 0.5 to 2
- obs_count: int32 [4, 8, 8], P('tm', 'tile'), may hold values from 10 to 32, as said below
Outputs:
- increment: float32 [4, 4, 2, 96, 1440], P('tm', None, None, 'tile')
Inputs may be any that keep to these rules, and one draw needn't show every extreme that they name: In every sub-window one tile, drawn from the seed, gets 32 filled slots from every source device; only the first obs_count slots of a block hold observations.
All inputs are finite; a program needn't handle non-finite values.
Results may differ from a plain program's by a relative error of at most 0.00002.
Values sent between devices are 32-bit elements; how exact they have to be, the bound alone decides.
No kernel may reach another device: no remote copies, remote signals or barrier semaphores. Data moves between devices by JAX's collectives and lax.ppermute only.
A program may use at most 128 MiB of HBM per device.

v0:
```python
import functools

import jax
import jax.numpy as jnp
from jax import lax
from jax.experimental import pallas as pl
from jax.experimental.pallas import tpu as pltpu
from jax.sharding import PartitionSpec as P

STEPS = 2
ITERS = 2
CHAINS = 3
LANES = 128
VMEM_LIMIT = 48 * 1024 * 1024


def padded(block, sides, width):
    for axis, dim in sides:
        count = lax.axis_size(axis)
        forward = [(i, i + 1) for i in range(count - 1)]
        backward = [(target, source) for source, target in forward]
        low = lax.ppermute(
            lax.slice_in_dim(block, block.shape[dim] - width, None, axis=dim), axis, forward
        )
        high = lax.ppermute(lax.slice_in_dim(block, 0, width, axis=dim), axis, backward)
        block = jnp.concatenate([low, block, high], axis=dim)
    return block


def shifted(value, axis, steps):
    count = lax.axis_size(axis)
    first, last = (max(0, -steps), min(count, count - steps))
    return lax.ppermute(value, axis, [(source, source + steps) for source in range(first, last)])


def apply_step(field, coef, adjoint):
    east_c = coef[0]
    north_c = coef[1]
    diff_c = coef[2]
    if adjoint:
        to_east = (diff_c - 0.5 * east_c) * field
        to_west = (diff_c + 0.5 * east_c) * field
        to_north = (diff_c - 0.5 * north_c) * field
        to_south = (diff_c + 0.5 * north_c) * field
        middle = (1.0 - 4.0 * diff_c[:, 1:-1]) * field[:, :, 1:-1]
        return (
            middle
            + jnp.roll(to_east[:, :, 1:-1], 1, axis=-1)
            + jnp.roll(to_west[:, :, 1:-1], -1, axis=-1)
            + to_north[:, :, :-2]
            + to_south[:, :, 2:]
        )
    inner = field[:, :, 1:-1]
    diff_in = diff_c[:, 1:-1]
    east_in = east_c[:, 1:-1]
    north_in = north_c[:, 1:-1]
    return (
        (1.0 - 4.0 * diff_in) * inner
        + (diff_in - 0.5 * east_in) * jnp.roll(inner, -1, axis=-1)
        + (diff_in + 0.5 * east_in) * jnp.roll(inner, 1, axis=-1)
        + (diff_in - 0.5 * north_in) * field[:, :, 2:]
        + (diff_in + 0.5 * north_in) * field[:, :, :-2]
    )


def advance(field, coef, adjoint):
    for repeat in range(STEPS):
        extended = padded(field, (("tile", 2),), 1)
        field = apply_step(extended, coef, adjoint)
    return field


def per_device(
    advect_east, advect_north, diffusion, background_var, obs_cell, obs_value, obs_weight, obs_count
):
    windows_count = lax.axis_size("tm")
    tiles = lax.axis_size("tile")
    coefs = jnp.stack([advect_east[0], advect_north[0], diffusion[0]])
    coef_ext = padded(coefs, (("tile", 2),), 1)
    cells = obs_cell.reshape(tiles, -1)
    slot_count = cells.shape[1]
    live = jnp.arange(slot_count, dtype=jnp.int32)[None, :] < obs_count.reshape(tiles)[:, None]
    masked = obs_weight.reshape(tiles, -1) * live.astype(jnp.float32)
    received = lax.all_to_all(
        jnp.stack([obs_value.reshape(tiles, -1), masked]),
        "tile",
        split_axis=1,
        concat_axis=1,
        tiled=True,
    )
    received_cells = lax.all_to_all(cells, "tile", split_axis=0, concat_axis=0, tiled=True)
    departures = received[0].reshape(-1)
    obs_weights = received[1].reshape(-1)
    flat_cells = received_cells.reshape(-1)
    local_var = background_var[0]
    state_shape = local_var.shape
    cell_total = state_shape[0] * state_shape[1] * state_shape[2] * state_shape[3]
    increment = jnp.zeros(state_shape, jnp.float32)
    for iteration in range(ITERS):
        if iteration == 0:
            innov = obs_weights * (0.0 - departures)
        else:
            forward_carried = advance(increment, coef_ext, False)
            for forward_window in range(windows_count - 1):
                forward_incoming = shifted(forward_carried, "tm", 1)
                forward_carried = advance(forward_incoming + increment, coef_ext, False)
            innov = obs_weights * (
                jnp.take(forward_carried.reshape(cell_total), flat_cells, axis=0) - departures
            )
        gridded = jnp.zeros((cell_total,), jnp.float32).at[flat_cells].add(innov)
        source = gridded.reshape(state_shape)
        carried = advance(source, coef_ext, True)
        for window in range(windows_count - 1):
            incoming = shifted(carried, "tm", -1)
            carried = advance(incoming + source, coef_ext, True)
        increment = increment - 0.5 * (increment + local_var * carried)
    return increment[None]


class Plan:
    def __init__(self, mesh_shape, var_shape, slot_shape):
        self.subs, self.tiles = mesh_shape["tm"], mesh_shape["tile"]
        self.count = self.subs * self.tiles
        _, self.vars, self.lev, self.nlat, self.lon = var_shape
        self.lat = self.nlat // self.tiles
        self.slots = slot_shape[2] // self.tiles
        self.cols = self.count // self.lev
        self.width = self.lon // self.cols
        self.half = self.width // 2
        self.halo = CHAINS * STEPS * self.subs
        self.margin = (LANES - self.width) // 2
        self.extra = self.halo - self.margin
        self.span = self.width + 2 * self.halo
        self.coef_row = self.lat * self.vars
        self.obs_row = self.coef_row + 3 * self.lat
        self.rows = self.obs_row + 6
        self.pitch = self.nlat + STEPS
        self.wide = -(-self.extra // STEPS)
        self.area = self.nlat * self.vars

    def borrows(self, k):
        return (CHAINS - 1) * STEPS * self.subs + STEPS * (k + 1) > self.margin

    def fits(self):
        if self.count % self.lev or self.lon % self.cols or self.width % 2:
            return False
        for k in range(self.subs):
            spare = self.margin - STEPS * (2 * self.subs - k)
            if spare < 0 or (self.borrows(k) and spare < self.extra):
                return False
        return (
            self.half + 2 * self.halo <= LANES
            and 0 <= self.extra <= 16
            and self.vars == 4
            and self.lat % 2 == 0
            and 0 < self.wide < self.subs
            and self.tiles == 8
            and self.slots & (self.slots - 1) == 0
            and self.slots * self.tiles == 2 * LANES
            and self.width + 2 * self.margin == LANES
            and self.width * self.vars <= 3 * LANES
            and self.count * self.rows % 8 == 0
            and self.rows % 2 == 0
        )


def pack_kernel(
    plan, count_ref, cell_ref, value_ref, weight_ref, east_ref, north_ref, diff_ref, var_ref, out_ref, wide
):
    p = plan
    pad = 2 * LANES
    right = wide.shape[-1] - pad - p.lon
    per_level = p.vars + 3

    def fill(z, carry):
        for v in range(per_level):
            field = var_ref[v, z] if v < p.vars else (east_ref, north_ref, diff_ref)[v - p.vars][z]
            at = z * per_level + v
            wide[at, :, pad : pad + p.lon] = field
            wide[at, :, :pad] = field[:, p.lon - pad :]
            wide[at, :, pad + p.lon :] = field[:, :right]
        return carry

    lax.fori_loop(0, p.lev, fill, 0)

    lane = lax.broadcasted_iota(jnp.int32, (1, p.tiles * p.slots), 1)
    filled = jnp.zeros_like(lane)
    for t in range(p.tiles):
        filled = jnp.where(lane >= t * p.slots, count_ref[0, t], filled)
    weight = jnp.where((lane & (p.slots - 1)) < filled, weight_ref[...], 0.0)
    obs = []
    for x in (weight, weight * value_ref[...], cell_ref[...].astype(jnp.float32)):
        obs += [x[:, :LANES], x[:, LANES:]]
    obs = jnp.concatenate(obs, axis=0)
    lanes = lax.broadcasted_iota(jnp.int32, (p.lat, LANES), 1)
    borrows = jnp.where(p.borrows(lax.axis_index("tm")), p.extra, 0)

    def blocks(z, carry):
        for j in range(p.cols):
            first = pad + j * p.width - p.margin
            tile, low = divmod(first, LANES)

            def moved(a, t):
                x = wide[z * per_level + a, :, t * LANES : (t + 1) * LANES]
                return pltpu.roll(x, LANES - low, 1)

            base = (z * p.cols + j) * p.rows
            for v in range(p.vars):
                piece = jnp.where(lanes < LANES - low, moved(v, tile), moved(v, tile + 1))
                if v < 3:
                    here, after = moved(p.vars + v, tile), moved(p.vars + v, tile + 1)
                    rows = pl.ds(base + p.coef_row + v * p.lat, p.lat)
                    out_ref[rows, :] = jnp.where(lanes < LANES - low, here, after)
                    if low < p.extra:
                        here = jnp.where(lanes < LANES - low, moved(p.vars + v, tile - 1), here)
                    if low + p.extra > LANES:
                        after = jnp.where(lanes < LANES - low, after, moved(p.vars + v, tile + 2))
                    piece = jnp.where(lanes < borrows, after, piece)
                    piece = jnp.where(lanes >= LANES - borrows, here, piece)
                out_ref[pl.ds(base + v, p.lat, stride=p.vars), :] = piece
            out_ref[pl.ds(base + p.obs_row, 6), :] = obs
        return carry

    lax.fori_loop(0, p.lev, blocks, 0)


class Stores:
    def __init__(self):
        self.held = []

    def put(self, ref, at, value):
        self.held.append((ref, at, value))

    def flush(self):
        for ref, at, value in self.held:
            ref[at] = value
        self.held = []


def looped(count, unroll, body):
    def many(i, carry):
        stores = Stores()
        for u in range(unroll):
            body(i * unroll + u, stores)
        stores.flush()
        return carry

    lax.fori_loop(0, count // unroll, many, 0)


def swap_blocks(x, slots):
    size = x.shape[0]
    sub = lax.broadcasted_iota(jnp.int32, x.shape, 0)
    block = lax.broadcasted_iota(jnp.int32, x.shape, 1) >> (slots.bit_length() - 1)
    out = x
    for d in range(1, size):
        moved = pltpu.roll(pltpu.roll(x, size - d, 0), d * slots, 1)
        out = jnp.where(block == ((sub + d) & (size - 1)), moved, out)
    return out


def spread(a, b, count):
    return (
        jnp.concatenate([a[:count], b[:count]], axis=0),
        jnp.concatenate([a[count:], b[count:]], axis=0),
    )


def chain_kernel(
    plan,
    recv_ref,
    out_ref,
    mid_w,
    east_w,
    west_w,
    north_w,
    south_w,
    source_w,
    result_w,
    carried_w,
    mid_c,
    east_c,
    west_c,
    north_c,
    south_c,
    weight_g,
    innov,
    results,
    carried,
    obs_tab,
):
    p = plan
    f32 = jnp.float32
    me = lax.axis_index("tm") * p.tiles + lax.axis_index("tile")
    level = (me // p.cols).astype(f32)
    origin = ((me % p.cols) * p.width - p.halo).astype(f32)
    two = 2 * p.vars
    shape = (two, LANES)
    sub = lax.broadcasted_iota(jnp.int32, shape, 0)
    lane = lax.broadcasted_iota(jnp.int32, shape, 1)
    lower = sub < p.vars
    in_half = lane < p.margin + p.half
    n = p.nlat
    pitch = p.pitch
    area = p.area
    whole = p.subs * area
    nothing = ITERS * whole
    lead = two
    low_wide = p.subs - p.wide
    zero = jnp.zeros(shape, f32)

    def rows8(start):
        return pl.ds(pl.multiple_of(start, two), two)

    def clear(ref, start, count):
        def body(i, carry):
            for u in range(8):
                ref[rows8(start + (i * 8 + u) * two), :] = zero
            return carry

        lax.fori_loop(0, count // (8 * two), body, 0)

    clear(innov, nothing, area)
    clear(results, nothing, area)
    for ref in (mid_c, east_c, west_c, north_c, south_c, carried):
        ref[:lead, :] = zero
        ref[ref.shape[0] - lead :, :] = zero
    for k in range(p.wide):
        for l in range(n, pitch):
            for ref in (mid_w, east_w, west_w, north_w, south_w, source_w):
                ref[k * pitch + l] = zero
    for l in range(n, pitch):
        carried_w[l * two : (l + 1) * two, :] = zero

    def observe(k, stores):
        raw = []
        for i in range(6):
            raw.append(recv_ref[pl.ds(k * p.tiles * p.rows + p.obs_row + i, p.tiles, stride=p.rows), :])
        w, wy, cell = (jnp.concatenate(raw[2 * i : 2 * i + 2], axis=1) for i in range(3))
        w, wy, cell = (swap_blocks(x, p.slots) for x in (w, wy, cell))
        row = jnp.floor((cell + 0.5) * (1.0 / p.lon))
        lon = cell - row * p.lon
        group = jnp.floor((row + 0.5) * (1.0 / p.lat))
        lat = row - group * p.lat
        var = jnp.floor((group + 0.5) * (1.0 / p.lev))
        lev = group - var * p.lev
        at = lon - origin
        at = jnp.where(at < 0, at + p.lon, at)
        at = jnp.where(at >= p.lon, at - p.lon, at)
        place = at - p.extra
        here = (lev == level) & (at < p.span)
        main = here & (place >= 0) & (place < LANES)
        outside = here & ~main
        around = jnp.where(place < 0, place + LANES, place - LANES)
        rows = pl.ds(k * p.tiles, p.tiles)
        stores.put(obs_tab, (0, rows), lat * p.vars + var)
        stores.put(obs_tab, (1, rows), jnp.where(main, place, -1.0))
        stores.put(obs_tab, (2, rows), jnp.where(outside, around, -1.0))
        for i, x in ((3, w), (6, -wy)):
            one = x.astype(jnp.bfloat16).astype(f32)
            two = (x - one).astype(jnp.bfloat16).astype(f32)
            stores.put(obs_tab, (i, rows), one)
            stores.put(obs_tab, (i + 1, rows), two)
            stores.put(obs_tab, (i + 2, rows), x - one - two)

    looped(p.subs, 1, observe)

    n_rows = p.lat * p.vars
    slots = p.tiles * p.slots
    row_id = lax.broadcasted_iota(jnp.int32, (n_rows, slots), 0).astype(f32)
    lane_id = lax.broadcasted_iota(jnp.int32, (LANES, slots), 0).astype(f32)
    row_lane = lax.broadcasted_iota(jnp.int32, (n_rows, LANES), 1)

    def wide_tile(kt):
        return jnp.maximum(kt - low_wide * p.tiles, kt % p.tiles)

    def row_of(kt):
        return kt * p.lat + kt // p.tiles * STEPS

    def grid(kt, stores):
        def entry(i):
            return obs_tab[i, pl.ds(kt, 1), :]

        def factor(rows, i):
            return jnp.where(lane_id[rows] == entry(i), 1.0, 0.0).astype(jnp.bfloat16)

        def product(first, right):
            left = [jnp.where(match, entry(first + q), 0.0).astype(jnp.bfloat16) for q in range(3)]
            left = jnp.concatenate(left, axis=0)
            full = lax.dot_general(left, right, (((1,), (1,)), ((), ())), preferred_element_type=f32)
            parts = [full[q * n_rows : (q + 1) * n_rows] for q in range(3)]
            return parts[0] + (parts[1] + parts[2])

        match = row_id == entry(0)
        main = factor(slice(0, LANES), 1)
        ends = [factor(slice(0, 16), 2), jnp.zeros((LANES - 32, slots), jnp.bfloat16), factor(slice(LANES - 16, LANES), 2)]
        at = (pl.ds(pl.multiple_of(kt * n_rows, two), n_rows),)
        stores.put(weight_g, at, product(3, main))
        summed = product(6, jnp.concatenate([main] + ends, axis=0))
        inside, outside = summed[:, :LANES], summed[:, LANES:]
        stores.put(innov, at, inside)
        left = jnp.where(row_lane >= LANES - p.extra, outside, inside)
        right = jnp.where(row_lane < p.extra, outside, inside)
        tile = wide_tile(kt)
        for pair in range(p.lat // 2):
            rows = slice(two * pair, two * (pair + 1))
            one, other = spread(left[rows], right[rows], p.vars)
            stores.put(source_w, row_of(tile) + 2 * pair, one)
            stores.put(source_w, row_of(tile) + 2 * pair + 1, other)

    def derive(got):
        east, north, diff = got
        east = 0.5 * east
        north = 0.5 * north
        return 1.0 - 4.0 * diff, diff - east, diff + east, diff - north, diff + north

    def one_row(at):
        return jnp.broadcast_to(recv_ref[pl.ds(at, 1), :], shape)

    edge_mask = (lower & (lane >= LANES - p.extra)) | (~lower & (lane < p.extra))

    def widen(kt, stores):
        base = kt * p.rows
        for l in range(p.lat):
            got = []
            for c in range(3):
                main = one_row(base + p.coef_row + c * p.lat + l)
                got.append(jnp.where(edge_mask, one_row(base + l * p.vars + c), main))
            for ref, value in zip((mid_w, east_w, west_w, north_w, south_w), derive(got)):
                stores.put(ref, row_of(wide_tile(kt)) + l, value)

    def double(kt, stores):
        base = kt * p.rows + p.coef_row
        for l in range(0, p.lat, 2):
            got = []
            for c in range(3):
                at = base + c * p.lat + l
                got.append(jnp.where(lower, one_row(at), one_row(at + 1)))
            at = rows8(lead + kt * n_rows + l * p.vars)
            for ref, value in zip((mid_c, east_c, west_c, north_c, south_c), derive(got)):
                stores.put(ref, (at,), value)

    def prepare(kt, stores):
        grid(kt, stores)
        double(kt, stores)
        widen(kt, stores)

    looped(p.count, 2, prepare)

    def wide_step(i, carry):
        k = p.wide - 1 - i // STEPS
        base = k * pitch
        starts = (i % STEPS == 0).astype(f32)
        stores = Stores()

        def terms(l):
            x = carried_w[l * two : (l + 1) * two, :] + starts * source_w[base + l]
            at = base + l
            here = (
                mid_w[at] * x
                + pltpu.roll(east_w[at] * x, 1, 1)
                + pltpu.roll(west_w[at] * x, LANES - 1, 1)
            )
            return here, north_w[at] * x, south_w[at] * x

        below = zero
        here, north, _ = terms(0)
        for l in range(n):
            now, next_north, south = terms(l + 1)
            y = here + below + south
            here, below, north = now, north, next_north
            stores.put(carried_w, (slice(l * two, (l + 1) * two),), y)
            stores.put(result_w, (rows8((k * n + l) * two),), y)
        stores.flush()
        return carry

    def narrow(ref, at):
        mixed = ref[pl.ds(at + p.vars, two), :]
        left = jnp.where(lower, ref[pl.ds(at, two), :], mixed)
        right = jnp.where(lower, mixed, ref[pl.ds(at + two, two), :])
        return jnp.where(in_half, left, right)

    def narrow_results(i, stores):
        stores.put(results, (rows8(low_wide * area + i * two),), narrow(result_w, i * 2 * two))

    def narrow_carried(i, stores):
        value = narrow(carried_w, i * 2 * two) + innov[rows8((low_wide - 1) * area + i * two), :]
        stores.put(carried, (rows8(lead + i * two),), value)

    def begin_adjoint(i, stores):
        stores.put(carried, (rows8(lead + i * two),), innov[rows8(whole + (p.subs - 1) * area + i * two), :])

    def scaled(k, tile, q, at):
        var = recv_ref[pl.ds((k * p.tiles + tile) * p.rows + q * two, two), :]
        return 0.5 * (var * results[at, :])

    def begin_forward(tile, stores):
        for q in range(p.lat // 2):
            at = tile * n_rows + q * two
            stores.put(carried, (rows8(lead + at),), -scaled(0, tile, q, rows8(at)))

    def near(ref, base, at, shift):
        return ref[pl.ds(base + at + lead + shift * p.vars, two), :]

    def adjoint_step(i, phase):
        k = p.subs - 1 - i // STEPS
        base = k * area
        into = phase * whole + base
        ends = (i % STEPS == STEPS - 1) & (k > 0)
        source = jnp.where(ends, into - area, nothing)
        stores = Stores()
        for at in range(0, area, two):
            x = near(carried, 0, at, 0)
            y = (
                near(mid_c, base, at, 0) * x
                + pltpu.roll(near(east_c, base, at, 0) * x, 1, 1)
                + pltpu.roll(near(west_c, base, at, 0) * x, LANES - 1, 1)
                + near(north_c, base, at, -1) * near(carried, 0, at, -1)
                + near(south_c, base, at, 1) * near(carried, 0, at, 1)
            )
            stores.put(results, (rows8(into + at),), y)
            stores.put(carried, (slice(lead + at, lead + at + two),), y + innov[rows8(source + at), :])
        stores.flush()
        return phase

    def forward_step(i, carry):
        k = i // STEPS
        base = k * area
        ends = (i % STEPS == STEPS - 1) & (k < p.subs - 1)
        source = jnp.where(ends, base + area, nothing)
        later = jnp.minimum(k + 1, p.subs - 1)
        stores = Stores()
        for at in range(0, area, two):
            x = near(carried, 0, at, 0)
            y = (
                near(mid_c, base, at, 0) * x
                + near(east_c, base, at, 0) * pltpu.roll(x, LANES - 1, 1)
                + near(west_c, base, at, 0) * pltpu.roll(x, 1, 1)
                + near(north_c, base, at, 0) * near(carried, 0, at, 1)
                + near(south_c, base, at, 0) * near(carried, 0, at, -1)
            )
            here = rows8(base + at)
            stores.put(innov, (rows8(whole + base + at),), weight_g[here, :] * y + innov[here, :])
            force = scaled(later, at // n_rows, at % n_rows // two, rows8(source + at))
            stores.put(carried, (slice(lead + at, lead + at + two),), y - force)
        stores.flush()
        return carry

    def clear_wide(i, stores):
        stores.put(carried_w, (rows8(i * two),), zero)

    def iteration(phase, carry):
        @pl.when(phase == 0)
        def _():
            looped(n, 8, clear_wide)
            lax.fori_loop(0, p.wide * STEPS, wide_step, 0)
            looped(p.wide * n // 2, 12, narrow_results)
            looped(n // 2, 12, narrow_carried)

        @pl.when(phase > 0)
        def _():
            looped(n // 2, 12, begin_adjoint)

        lax.fori_loop(jnp.where(phase == 0, p.wide * STEPS, 0), p.subs * STEPS, adjoint_step, phase)

        @pl.when(phase < ITERS - 1)
        def _():
            looped(p.tiles, 2, begin_forward)
            lax.fori_loop(0, p.subs * STEPS, forward_step, 0)

        return carry

    lax.fori_loop(0, ITERS, iteration, 0)

    own = slice(p.margin, p.margin + p.width)

    def join(kt, stores):
        cols = []
        for v in range(p.vars):
            at = kt * n_rows + v
            early = results[pl.ds(at, p.lat, stride=p.vars), :]
            late = results[pl.ds(whole + at, p.lat, stride=p.vars), :]
            cols.append((0.5 * early + late)[:, own])
        spare = 3 * LANES - p.vars * p.width
        line = jnp.concatenate(cols + [jnp.zeros((p.lat, spare), f32)], axis=1)
        for i in range(3):
            at = (pl.ds(kt * p.lat * 3 + i, p.lat, stride=3),)
            stores.put(out_ref, at, line[:, i * LANES : (i + 1) * LANES])

    looped(p.count, 8, join)


def finish_kernel(plan, recv_ref, var_ref, out_ref):
    p = plan

    def level(z, carry):
        for j in range(p.cols):
            start = (z * p.cols + j) * p.lat * 3
            rows = [recv_ref[pl.ds(start + i, p.lat, stride=3), :] for i in range(3)]
            for v in range(p.vars):
                at, end = v * p.width, (v + 1) * p.width
                col = j * p.width
                while at < end:
                    i, low = divmod(at, LANES)
                    size = min(end - at, LANES - low)
                    cols = slice(col, col + size)
                    scale = -0.5 * var_ref[v, z, :, cols]
                    out_ref[v, z, :, cols] = scale * rows[i][:, low : low + size]
                    at, col = at + size, col + size
        return carry

    lax.fori_loop(0, p.lev, level, 0)


def transposed(
    plan, advect_east, advect_north, diffusion, background_var, obs_cell, obs_value, obs_weight, obs_count
):
    p = plan
    f32 = jnp.float32
    vmem = pl.BlockSpec(memory_space=pltpu.VMEM)
    params = pltpu.CompilerParams(vmem_limit_bytes=VMEM_LIMIT)
    var = background_var[0]
    packed = pl.pallas_call(
        functools.partial(pack_kernel, p),
        out_shape=jax.ShapeDtypeStruct((p.count * p.rows, LANES), f32),
        in_specs=[pl.BlockSpec(memory_space=pltpu.SMEM)] + [vmem] * 7,
        out_specs=vmem,
        scratch_shapes=[pltpu.VMEM(((p.vars + 3) * p.lev, p.lat, 15 * LANES), f32)],
        compiler_params=params,
        name="pack",
    )(
        obs_count.reshape(1, -1),
        obs_cell.reshape(1, -1),
        obs_value.reshape(1, -1),
        obs_weight.reshape(1, -1),
        advect_east[0],
        advect_north[0],
        diffusion[0],
        var,
    )
    received = lax.all_to_all(packed.reshape(-1, 2, LANES), ("tm", "tile"), 0, 0, tiled=True)
    received = received.reshape(-1, LANES)
    wide = pltpu.VMEM((p.wide * p.pitch, 2 * p.vars, LANES), f32)
    narrow = pltpu.VMEM((p.subs * p.area + 4 * p.vars, LANES), f32)
    both = pltpu.VMEM(((ITERS * p.subs + 1) * p.area, LANES), f32)
    back = pl.pallas_call(
        functools.partial(chain_kernel, p),
        out_shape=jax.ShapeDtypeStruct((p.count * p.lat * 3, LANES), f32),
        in_specs=[vmem],
        out_specs=vmem,
        scratch_shapes=[wide] * 6
        + [
            pltpu.VMEM((p.wide * p.nlat * 2 * p.vars, LANES), f32),
            pltpu.VMEM((p.pitch * 2 * p.vars, LANES), f32),
        ]
        + [narrow] * 5
        + [
            pltpu.VMEM((p.subs * p.area, LANES), f32),
            both,
            both,
            pltpu.VMEM((p.area + 4 * p.vars, LANES), f32),
            pltpu.VMEM((9, p.count, p.tiles * p.slots), f32),
        ],
        compiler_params=params,
        name="chains",
    )(received)
    back = back.reshape(-1, 4, LANES)
    returned = lax.all_to_all(back, ("tm", "tile"), 0, 0, tiled=True)
    returned = returned.reshape(-1, LANES)
    increment = pl.pallas_call(
        functools.partial(finish_kernel, p),
        out_shape=jax.ShapeDtypeStruct(var.shape, f32),
        in_specs=[vmem] * 2,
        out_specs=vmem,
        compiler_params=params,
        name="finish",
    )(returned, var)
    return increment[None]


def solution(mesh):
    def run(*args):
        plan = Plan(mesh.shape, args[3].shape, args[4].shape)
        work = functools.partial(transposed, plan) if plan.fits() else per_device
        return jax.shard_map(
            work,
            mesh=mesh,
            in_specs=(
                P("tm", None, "tile", None),
                P("tm", None, "tile", None),
                P("tm", None, "tile", None),
                P("tm", None, None, "tile", None),
                P("tm", "tile", None),
                P("tm", "tile", None),
                P("tm", "tile", None),
                P("tm", "tile", None),
            ),
            out_specs=P("tm", None, None, "tile", None),
            check_vma=False,
        )(*args)

    return run
```

profile of v0, /device:TPU:0, one launch (start us, length us, event | category | flops | bytes accessed | tf_op | source)
XLA Modules:
  0.0 82.1 jit_solution(3394689435539772738)
XLA Ops:
  0.0 0.0 copy-start.4
  0.0 0.0 copy-start.5
  0.0 0.0 copy-start.3
  0.0 0.0 copy-start.2
  0.0 0.0 copy-start.1
  0.0 0.0 copy-start
  0.0 1.0 %copy.19 = f32[1,2,12,1440]{3,2,1,0:T(8,128)S(1)} copy(f32[1,2,12,1440]{3,1,2,0:T(2,128)} %param.8) | data formatting | bytes 276480 | tf_op args[0]
  1.0 1.2 %copy.18 = f32[1,4,2,12,1440]{4,3,2,1,0:T(8,128)S(1)} copy(f32[1,4,2,12,1440]{4,2,3,1,0:T(2,128)} %param.11) | data formatting | bytes 1105920 | tf_op args[3]
  2.2 0.0 copy-done.4
  2.2 0.0 copy-done.5
  2.2 0.1 copy_bitcast_fusion.1
  2.3 0.0 copy-done.3
  2.3 0.0 copy-done.2
  2.3 0.0 copy-done.1
  2.3 0.0 copy-done
  2.3 1.9 %pack.1 = f32[2880,128]{1,0:T(8,128)S(1)} custom-call(s32[1,8]{1,0:T(1,128)S(1)} %bitcast.30, s32[1,256]{1,0:T(1,128)S(1)} %bitcast.27, f32[1,256]{1,0:T(1,128)S(1)} %bitcast.28, f32[1,256]{1,0:T(1,128)S(1)} %bitcast.29, f32[2,12,1440]{2,1,0:T(8,128)S(1)} %bitcast.26, f32[2,12,1440]{2,1,0:T(8,128)S(1)} %get-tuple-element.6.north_ref, ...), custom_call_target="tpu_custom_call" | custom-call | tf_op jit(solution)/shard_map/pack/pallas_call | solution.py:623
  4.3 43.8 %all_to_all.10 = f32[1440,2,128]{2,1,0:T(2,128)S(1)} all-to-all(f32[1440,2,128]{2,1,0:T(2,128)S(1)} %bitcast.21), channel_id=1, replica_groups=mesh['tm'=4,'tile'=8] {'tm','tile'}, dimensions={0} | all-to-all | bytes 2949120 | tf_op jit(solution)/shard_map/all_to_all | solution.py:641
  48.1 12.3 %chains.1 = f32[1152,128]{1,0:T(8,128)S(1)} custom-call(f32[2880,128]{1,0:T(8,128)S(1)} %bitcast.22), custom_call_target="tpu_custom_call" | custom-call | tf_op jit(solution)/shard_map/chains/pallas_call | solution.py:646
  60.4 19.9 %all_to_all.11 = f32[288,4,128]{2,1,0:T(4,128)S(1)} all-to-all(f32[288,4,128]{2,1,0:T(4,128)S(1)} %bitcast.25), channel_id=1, replica_groups=mesh['tm'=4,'tile'=8] {'tm','tile'}, dimensions={0} | all-to-all | bytes 1179648 | tf_op jit(solution)/shard_map/all_to_all | solution.py:668
  80.3 0.5 finish.1
  80.8 1.3 %copy.13 = f32[1,4,2,12,1440]{4,2,3,1,0:T(2,128)} copy(f32[1,4,2,12,1440]{4,3,2,1,0:T(8,128)S(1)} %bitcast.23) | data formatting | bytes 1105920 | tf_op jit(solution)/shard_map/broadcast_in_dim | solution.py:678
Async XLA Ops:
  0.0 2.2 %copy-start.4 = (f32[1,2,12,1440]{3,1,2,0:T(2,128)S(1)}, f32[1,2,12,1440]{3,1,2,0:T(2,128)}, u32[]{:S(2)}) copy-start(f32[1,2,12,1440]{3,1,2,0:T(2,128)} %param.10) | copy-start | bytes 414724
  0.0 2.2 %copy-start.5 = (f32[1,2,12,1440]{3,1,2,0:T(2,128)S(1)}, f32[1,2,12,1440]{3,1,2,0:T(2,128)}, u32[]{:S(2)}) copy-start(f32[1,2,12,1440]{3,1,2,0:T(2,128)} %param.9) | copy-start | bytes 414724
  0.0 2.3 %copy-start.3 = (s32[1,1,8]{2,1,0:T(1,128)S(1)}, s32[1,1,8]{2,1,0:T(1,128)}, u32[]{:S(2)}) copy-start(s32[1,1,8]{2,1,0:T(1,128)} %param.15) | copy-start | bytes 100
  0.0 2.3 %copy-start.2 = (f32[1,1,256]{2,1,0:T(1,128)S(1)}, f32[1,1,256]{2,1,0:T(1,128)}, u32[]{:S(2)}) copy-start(f32[1,1,256]{2,1,0:T(1,128)} %param.14) | copy-start | bytes 3076
  0.0 2.3 %copy-start.1 = (f32[1,1,256]{2,1,0:T(1,128)S(1)}, f32[1,1,256]{2,1,0:T(1,128)}, u32[]{:S(2)}) copy-start(f32[1,1,256]{2,1,0:T(1,128)} %param.13) | copy-start | bytes 3076
  0.0 2.3 %copy-start = (s32[1,1,256]{2,1,0:T(1,128)S(1)}, s32[1,1,256]{2,1,0:T(1,128)}, u32[]{:S(2)}) copy-start(s32[1,1,256]{2,1,0:T(1,128)} %param.12) | copy-start | bytes 3076
where the time goes:
time: 82.3 us; the launch traced here: 82.1 us
  blocking collectives  63.7 us (77%)
  Pallas kernels  14.8 us (18%)
  local copies, waits for them, and re-layouts  3.53 us (4%)
    all_to_all x1, blocking collectives, transposed(): lax.all_to_all(packed.reshape(-1, 2, LANES), ('tm', 'tile'), 0, 0, tiled=...  43.8 us
    all_to_all x1, blocking collectives, transposed(): returned = lax.all_to_all(back, ('tm', 'tile'), 0, 0, tiled=True)  19.9 us
    pallas_call x1, Pallas kernels, transposed(): pl.pallas_call(functools.partial(chain_kernel, p), out_shape=jax.ShapeDty...  12.3 us
    unnamed x14, local copies, waits for them, and re-layouts  2.2 us
    pallas_call x1, Pallas kernels, transposed(): pl.pallas_call(functools.partial(pack_kernel, p), out_shape=jax.ShapeDtyp...  1.94 us

commit v1 on v0

--- a/solution.py
+++ b/solution.py
@@ -445,7 +445,7 @@
         double(kt, stores)
         widen(kt, stores)
 
-    looped(p.count, 2, prepare)
+    looped(p.count, 4, prepare)
 
     def wide_step(i, carry):
         k = p.wide - 1 - i // STEPS
@@ -587,7 +587,7 @@
             at = (pl.ds(kt * p.lat * 3 + i, p.lat, stride=3),)
             stores.put(out_ref, at, line[:, i * LANES : (i + 1) * LANES])
 
-    looped(p.count, 8, join)
+    looped(p.count, 4, join)
 
 
 def finish_kernel(plan, recv_ref, var_ref, out_ref):

time: 82.3 us -> 81.3 us (0.988)
  Pallas kernels: 14.8 us -> 13.8 us
    pallas_call x1, Pallas kernels: 12.3 us -> 11.3 us  [transposed(): pl.pallas_call(functools.partial(chain_kernel, p), out_shape=jax.ShapeDty...]
where the time goes in v1:
time: 81.3 us; the launch traced here: 81.1 us
  blocking collectives  63.7 us (78%)
  Pallas kernels  13.8 us (17%)
  local copies, waits for them, and re-layouts  3.53 us (4%)
    all_to_all x1, blocking collectives, transposed(): lax.all_to_all(packed.reshape(-1, 2, LANES), ('tm', 'tile'), 0, 0, tiled=...  43.8 us
    all_to_all x1, blocking collectives, transposed(): returned = lax.all_to_all(back, ('tm', 'tile'), 0, 0, tiled=True)  19.8 us
    pallas_call x1, Pallas kernels, transposed(): pl.pallas_call(functools.partial(chain_kernel, p), out_shape=jax.ShapeDty...  11.3 us
    unnamed x14, local copies, waits for them, and re-layouts  2.2 us
    pallas_call x1, Pallas kernels, transposed(): pl.pallas_call(functools.partial(pack_kernel, p), out_shape=jax.ShapeDtyp...  1.94 us

profile of v1, /device:TPU:0, one launch (start us, length us, event | category | flops | bytes accessed | tf_op | source)
XLA Modules:
  0.0 81.1 jit_solution(10772222445146691534)
XLA Ops:
  0.0 0.0 copy-start.4
  0.0 0.0 copy-start.5
  0.0 0.0 copy-start.3
  0.0 0.0 copy-start.2
  0.0 0.0 copy-start.1
  0.0 0.0 copy-start
  0.0 1.0 %copy.19 = f32[1,2,12,1440]{3,2,1,0:T(8,128)S(1)} copy(f32[1,2,12,1440]{3,1,2,0:T(2,128)} %param.8) | data formatting | bytes 276480 | tf_op args[0]
  1.0 1.2 %copy.18 = f32[1,4,2,12,1440]{4,3,2,1,0:T(8,128)S(1)} copy(f32[1,4,2,12,1440]{4,2,3,1,0:T(2,128)} %param.11) | data formatting | bytes 1105920 | tf_op args[3]
  2.2 0.0 copy-done.4
  2.2 0.0 copy-done.5
  2.2 0.1 copy_bitcast_fusion.1
  2.3 0.0 copy-done.3
  2.3 0.0 copy-done.2
  2.3 0.0 copy-done.1
  2.3 0.0 copy-done
  2.3 1.9 %pack.1 = f32[2880,128]{1,0:T(8,128)S(1)} custom-call(s32[1,8]{1,0:T(1,128)S(1)} %bitcast.30, s32[1,256]{1,0:T(1,128)S(1)} %bitcast.27, f32[1,256]{1,0:T(1,128)S(1)} %bitcast.28, f32[1,256]{1,0:T(1,128)S(1)} %bitcast.29, f32[2,12,1440]{2,1,0:T(8,128)S(1)} %bitcast.26, f32[2,12,1440]{2,1,0:T(8,128)S(1)} %get-tuple-element.6.north_ref, ...), custom_call_target="tpu_custom_call" | custom-call | tf_op jit(solution)/shard_map/pack/pallas_call | solution.py:623
  4.3 43.8 %all_to_all.10 = f32[1440,2,128]{2,1,0:T(2,128)S(1)} all-to-all(f32[1440,2,128]{2,1,0:T(2,128)S(1)} %bitcast.21), channel_id=1, replica_groups=mesh['tm'=4,'tile'=8] {'tm','tile'}, dimensions={0} | all-to-all | bytes 2949120 | tf_op jit(solution)/shard_map/all_to_all | solution.py:641
  48.1 11.3 %chains.1 = f32[1152,128]{1,0:T(8,128)S(1)} custom-call(f32[2880,128]{1,0:T(8,128)S(1)} %bitcast.22), custom_call_target="tpu_custom_call" | custom-call | tf_op jit(solution)/shard_map/chains/pallas_call | solution.py:646
  59.5 19.8 %all_to_all.11 = f32[288,4,128]{2,1,0:T(4,128)S(1)} all-to-all(f32[288,4,128]{2,1,0:T(4,128)S(1)} %bitcast.25), channel_id=1, replica_groups=mesh['tm'=4,'tile'=8] {'tm','tile'}, dimensions={0} | all-to-all | bytes 1179648 | tf_op jit(solution)/shard_map/all_to_all | solution.py:668
  79.3 0.5 finish.1
  79.8 1.3 %copy.13 = f32[1,4,2,12,1440]{4,2,3,1,0:T(2,128)} copy(f32[1,4,2,12,1440]{4,3,2,1,0:T(8,128)S(1)} %bitcast.23) | data formatting | bytes 1105920 | tf_op jit(solution)/shard_map/broadcast_in_dim | solution.py:678
Async XLA Ops:
  0.0 2.2 %copy-start.4 = (f32[1,2,12,1440]{3,1,2,0:T(2,128)S(1)}, f32[1,2,12,1440]{3,1,2,0:T(2,128)}, u32[]{:S(2)}) copy-start(f32[1,2,12,1440]{3,1,2,0:T(2,128)} %param.10) | copy-start | bytes 414724
  0.0 2.2 %copy-start.5 = (f32[1,2,12,1440]{3,1,2,0:T(2,128)S(1)}, f32[1,2,12,1440]{3,1,2,0:T(2,128)}, u32[]{:S(2)}) copy-start(f32[1,2,12,1440]{3,1,2,0:T(2,128)} %param.9) | copy-start | bytes 414724
  0.0 2.3 %copy-start.3 = (s32[1,1,8]{2,1,0:T(1,128)S(1)}, s32[1,1,8]{2,1,0:T(1,128)}, u32[]{:S(2)}) copy-start(s32[1,1,8]{2,1,0:T(1,128)} %param.15) | copy-start | bytes 100
  0.0 2.3 %copy-start.2 = (f32[1,1,256]{2,1,0:T(1,128)S(1)}, f32[1,1,256]{2,1,0:T(1,128)}, u32[]{:S(2)}) copy-start(f32[1,1,256]{2,1,0:T(1,128)} %param.14) | copy-start | bytes 3076
  0.0 2.3 %copy-start.1 = (f32[1,1,256]{2,1,0:T(1,128)S(1)}, f32[1,1,256]{2,1,0:T(1,128)}, u32[]{:S(2)}) copy-start(f32[1,1,256]{2,1,0:T(1,128)} %param.13) | copy-start | bytes 3076
  0.0 2.3 %copy-start = (s32[1,1,256]{2,1,0:T(1,128)S(1)}, s32[1,1,256]{2,1,0:T(1,128)}, u32[]{:S(2)}) copy-start(s32[1,1,256]{2,1,0:T(1,128)} %param.12) | copy-start | bytes 3076

commit v2 on v1

--- a/solution.py
+++ b/solution.py
@@ -11,6 +11,7 @@
 ITERS = 2
 CHAINS = 3
 LANES = 128
+LAG = 12
 VMEM_LIMIT = 48 * 1024 * 1024
 
 
@@ -287,6 +288,7 @@
     innov,
     results,
     carried,
+    passed,
     obs_tab,
 ):
     p = plan
@@ -322,7 +324,7 @@
 
     clear(innov, nothing, area)
     clear(results, nothing, area)
-    for ref in (mid_c, east_c, west_c, north_c, south_c, carried):
+    for ref in (mid_c, east_c, west_c, north_c, south_c, carried, passed):
         ref[:lead, :] = zero
         ref[ref.shape[0] - lead :, :] = zero
     for k in range(p.wide):
@@ -502,47 +504,60 @@
     def near(ref, base, at, shift):
         return ref[pl.ds(base + at + lead + shift * p.vars, two), :]
 
-    def adjoint_step(i, phase):
-        k = p.subs - 1 - i // STEPS
-        base = k * area
-        into = phase * whole + base
-        ends = (i % STEPS == STEPS - 1) & (k > 0)
-        source = jnp.where(ends, into - area, nothing)
+    def adjoint_at(base, ref, at):
+        x = near(ref, 0, at, 0)
+        return (
+            near(mid_c, base, at, 0) * x
+            + pltpu.roll(near(east_c, base, at, 0) * x, 1, 1)
+            + pltpu.roll(near(west_c, base, at, 0) * x, LANES - 1, 1)
+            + near(north_c, base, at, -1) * near(ref, 0, at, -1)
+            + near(south_c, base, at, 1) * near(ref, 0, at, 1)
+        )
+
+    def forward_at(base, ref, at):
+        x = near(ref, 0, at, 0)
+        return (
+            near(mid_c, base, at, 0) * x
+            + near(east_c, base, at, 0) * pltpu.roll(x, LANES - 1, 1)
+            + near(west_c, base, at, 0) * pltpu.roll(x, 1, 1)
+            + near(north_c, base, at, 0) * near(ref, 0, at, 1)
+            + near(south_c, base, at, 0) * near(ref, 0, at, -1)
+        )
+
+    def window(one, base, last):
+        for at in range(0, area + LAG * two, two):
+            if at < area:
+                passed[lead + at : lead + at + two, :] = one(base, carried, at)
+            at -= LAG * two
+            if at >= 0:
+                carried[lead + at : lead + at + two, :] = last(at, one(base, passed, at))
+
+    def adjoint_window(i, phase):
+        k = p.subs - 1 - i
+        into = phase * whole + k * area
+        source = jnp.where(k > 0, into - area, nothing)
         stores = Stores()
-        for at in range(0, area, two):
-            x = near(carried, 0, at, 0)
-            y = (
-                near(mid_c, base, at, 0) * x
-                + pltpu.roll(near(east_c, base, at, 0) * x, 1, 1)
-                + pltpu.roll(near(west_c, base, at, 0) * x, LANES - 1, 1)
-                + near(north_c, base, at, -1) * near(carried, 0, at, -1)
-                + near(south_c, base, at, 1) * near(carried, 0, at, 1)
-            )
+
+        def last(at, y):
             stores.put(results, (rows8(into + at),), y)
-            stores.put(carried, (slice(lead + at, lead + at + two),), y + innov[rows8(source + at), :])
+            return y + innov[rows8(source + at), :]
+
+        window(adjoint_at, k * area, last)
         stores.flush()
         return phase
 
-    def forward_step(i, carry):
-        k = i // STEPS
+    def forward_window(k, carry):
         base = k * area
-        ends = (i % STEPS == STEPS - 1) & (k < p.subs - 1)
-        source = jnp.where(ends, base + area, nothing)
+        source = jnp.where(k < p.subs - 1, base + area, nothing)
         later = jnp.minimum(k + 1, p.subs - 1)
         stores = Stores()
-        for at in range(0, area, two):
-            x = near(carried, 0, at, 0)
-            y = (
-                near(mid_c, base, at, 0) * x
-                + near(east_c, base, at, 0) * pltpu.roll(x, LANES - 1, 1)
-                + near(west_c, base, at, 0) * pltpu.roll(x, 1, 1)
-                + near(north_c, base, at, 0) * near(carried, 0, at, 1)
-                + near(south_c, base, at, 0) * near(carried, 0, at, -1)
-            )
+
+        def last(at, y):
             here = rows8(base + at)
             stores.put(innov, (rows8(whole + base + at),), weight_g[here, :] * y + innov[here, :])
-            force = scaled(later, at // n_rows, at % n_rows // two, rows8(source + at))
-            stores.put(carried, (slice(lead + at, lead + at + two),), y - force)
+            return y - scaled(later, at // n_rows, at % n_rows // two, rows8(source + at))
+
+        window(forward_at, base, last)
         stores.flush()
         return carry
 
@@ -561,12 +576,12 @@
         def _():
             looped(n // 2, 12, begin_adjoint)
 
-        lax.fori_loop(jnp.where(phase == 0, p.wide * STEPS, 0), p.subs * STEPS, adjoint_step, phase)
+        lax.fori_loop(jnp.where(phase == 0, p.wide, 0), p.subs, adjoint_window, phase)
 
         @pl.when(phase < ITERS - 1)
         def _():
             looped(p.tiles, 2, begin_forward)
-            lax.fori_loop(0, p.subs * STEPS, forward_step, 0)
+            lax.fori_loop(0, p.subs, forward_window, 0)
 
         return carry
 
@@ -659,6 +674,7 @@
             both,
             both,
             pltpu.VMEM((p.area + 4 * p.vars, LANES), f32),
+            pltpu.VMEM((p.area + 4 * p.vars, LANES), f32),
             pltpu.VMEM((9, p.count, p.tiles * p.slots), f32),
         ],
         compiler_params=params,

time: 81.3 us -> 80.9 us (level)
  no operation moved by 1% of the time
where the time goes in v2:
time: 80.9 us; the launch traced here: 80.8 us
  blocking collectives  63.7 us (79%)
  Pallas kernels  13.4 us (17%)
  local copies, waits for them, and re-layouts  3.53 us (4%)
    all_to_all x1, blocking collectives, transposed(): lax.all_to_all(packed.reshape(-1, 2, LANES), ('tm', 'tile'), 0, 0, tiled=...  43.8 us
    all_to_all x1, blocking collectives, transposed(): returned = lax.all_to_all(back, ('tm', 'tile'), 0, 0, tiled=True)  19.8 us
    pallas_call x1, Pallas kernels, transposed(): pl.pallas_call(functools.partial(chain_kernel, p), out_shape=jax.ShapeDty...  11 us
    unnamed x14, local copies, waits for them, and re-layouts  2.2 us
    pallas_call x1, Pallas kernels, transposed(): pl.pallas_call(functools.partial(pack_kernel, p), out_shape=jax.ShapeDtyp...  1.94 us

profile of v2, /device:TPU:0, one launch (start us, length us, event | category | flops | bytes accessed | tf_op | source)
XLA Modules:
  0.0 80.8 jit_solution(4740201861684339678)
XLA Ops:
  0.0 0.0 copy-start.4
  0.0 0.0 copy-start.5
  0.0 0.0 copy-start.3
  0.0 0.0 copy-start.2
  0.0 0.0 copy-start.1
  0.0 0.0 copy-start
  0.0 1.0 %copy.19 = f32[1,2,12,1440]{3,2,1,0:T(8,128)S(1)} copy(f32[1,2,12,1440]{3,1,2,0:T(2,128)} %param.8) | data formatting | bytes 276480 | tf_op args[0]
  1.0 1.2 %copy.18 = f32[1,4,2,12,1440]{4,3,2,1,0:T(8,128)S(1)} copy(f32[1,4,2,12,1440]{4,2,3,1,0:T(2,128)} %param.11) | data formatting | bytes 1105920 | tf_op args[3]
  2.2 0.0 copy-done.4
  2.2 0.0 copy-done.5
  2.2 0.1 copy_bitcast_fusion.1
  2.3 0.0 copy-done.3
  2.3 0.0 copy-done.2
  2.3 0.0 copy-done.1
  2.3 0.0 copy-done
  2.3 1.9 %pack.1 = f32[2880,128]{1,0:T(8,128)S(1)} custom-call(s32[1,8]{1,0:T(1,128)S(1)} %bitcast.30, s32[1,256]{1,0:T(1,128)S(1)} %bitcast.27, f32[1,256]{1,0:T(1,128)S(1)} %bitcast.28, f32[1,256]{1,0:T(1,128)S(1)} %bitcast.29, f32[2,12,1440]{2,1,0:T(8,128)S(1)} %bitcast.26, f32[2,12,1440]{2,1,0:T(8,128)S(1)} %get-tuple-element.6.north_ref, ...), custom_call_target="tpu_custom_call" | custom-call | tf_op jit(solution)/shard_map/pack/pallas_call | solution.py:638
  4.3 43.8 %all_to_all.10 = f32[1440,2,128]{2,1,0:T(2,128)S(1)} all-to-all(f32[1440,2,128]{2,1,0:T(2,128)S(1)} %bitcast.21), channel_id=1, replica_groups=mesh['tm'=4,'tile'=8] {'tm','tile'}, dimensions={0} | all-to-all | bytes 2949120 | tf_op jit(solution)/shard_map/all_to_all | solution.py:656
  48.1 11.0 %chains.1 = f32[1152,128]{1,0:T(8,128)S(1)} custom-call(f32[2880,128]{1,0:T(8,128)S(1)} %bitcast.22), custom_call_target="tpu_custom_call" | custom-call | tf_op jit(solution)/shard_map/chains/pallas_call | solution.py:661
  59.1 19.8 %all_to_all.11 = f32[288,4,128]{2,1,0:T(4,128)S(1)} all-to-all(f32[288,4,128]{2,1,0:T(4,128)S(1)} %bitcast.25), channel_id=1, replica_groups=mesh['tm'=4,'tile'=8] {'tm','tile'}, dimensions={0} | all-to-all | bytes 1179648 | tf_op jit(solution)/shard_map/all_to_all | solution.py:684
  79.0 0.5 finish.1
  79.5 1.3 %copy.13 = f32[1,4,2,12,1440]{4,2,3,1,0:T(2,128)} copy(f32[1,4,2,12,1440]{4,3,2,1,0:T(8,128)S(1)} %bitcast.23) | data formatting | bytes 1105920 | tf_op jit(solution)/shard_map/broadcast_in_dim | solution.py:694
Async XLA Ops:
  0.0 2.2 %copy-start.4 = (f32[1,2,12,1440]{3,1,2,0:T(2,128)S(1)}, f32[1,2,12,1440]{3,1,2,0:T(2,128)}, u32[]{:S(2)}) copy-start(f32[1,2,12,1440]{3,1,2,0:T(2,128)} %param.10) | copy-start | bytes 414724
  0.0 2.2 %copy-start.5 = (f32[1,2,12,1440]{3,1,2,0:T(2,128)S(1)}, f32[1,2,12,1440]{3,1,2,0:T(2,128)}, u32[]{:S(2)}) copy-start(f32[1,2,12,1440]{3,1,2,0:T(2,128)} %param.9) | copy-start | bytes 414724
  0.0 2.3 %copy-start.3 = (s32[1,1,8]{2,1,0:T(1,128)S(1)}, s32[1,1,8]{2,1,0:T(1,128)}, u32[]{:S(2)}) copy-start(s32[1,1,8]{2,1,0:T(1,128)} %param.15) | copy-start | bytes 100
  0.0 2.3 %copy-start.2 = (f32[1,1,256]{2,1,0:T(1,128)S(1)}, f32[1,1,256]{2,1,0:T(1,128)}, u32[]{:S(2)}) copy-start(f32[1,1,256]{2,1,0:T(1,128)} %param.14) | copy-start | bytes 3076
  0.0 2.3 %copy-start.1 = (f32[1,1,256]{2,1,0:T(1,128)S(1)}, f32[1,1,256]{2,1,0:T(1,128)}, u32[]{:S(2)}) copy-start(f32[1,1,256]{2,1,0:T(1,128)} %param.13) | copy-start | bytes 3076
  0.0 2.3 %copy-start = (s32[1,1,256]{2,1,0:T(1,128)S(1)}, s32[1,1,256]{2,1,0:T(1,128)}, u32[]{:S(2)}) copy-start(s32[1,1,256]{2,1,0:T(1,128)} %param.12) | copy-start | bytes 3076

commit v3 on v2

--- a/solution.py
+++ b/solution.py
@@ -12,6 +12,7 @@
 CHAINS = 3
 LANES = 128
 LAG = 12
+PACK_LIMIT = 55 * 1024 * 1024
 VMEM_LIMIT = 48 * 1024 * 1024
 
 
@@ -165,29 +166,50 @@
         )
 
 
-def pack_kernel(
-    plan, count_ref, cell_ref, value_ref, weight_ref, east_ref, north_ref, diff_ref, var_ref, out_ref, wide
-):
+def fetch(sources, targets, sems):
+    copies = [pltpu.make_async_copy(x, y, sems.at[i]) for i, (x, y) in enumerate(zip(sources, targets))]
+    for copy in copies:
+        copy.start()
+    return copies
+
+
+def pack_kernel(plan, *refs):
     p = plan
+    sources, (out_hbm, wide, out_ref), targets, sems, out_sems = refs[:8], refs[8:11], refs[11:19], refs[19], refs[20]
+    copies = fetch(sources, targets, sems)
+    count_ref, cell_ref, value_ref, weight_ref, east_ref, north_ref, diff_ref, var_ref = targets
+    for copy in copies:
+        copy.wait()
     pad = 2 * LANES
     right = wide.shape[-1] - pad - p.lon
     per_level = p.vars + 3
 
-    def fill(z, carry):
-        for v in range(per_level):
-            field = var_ref[v, z] if v < p.vars else (east_ref, north_ref, diff_ref)[v - p.vars][z]
-            at = z * per_level + v
-            wide[at, :, pad : pad + p.lon] = field
-            wide[at, :, :pad] = field[:, p.lon - pad :]
-            wide[at, :, pad + p.lon :] = field[:, :right]
-        return carry
-
-    lax.fori_loop(0, p.lev, fill, 0)
+    def fill(v, field):
+        for low in range(0, p.lon, LANES):
+            size = min(LANES, p.lon - low)
+            both = jnp.swapaxes(field[:, :, low : low + size], 0, 1)
+            for z in range(p.lev):
+                wide[z * per_level + v, :, pad + low : pad + low + size] = both[z]
+
+    def fill_var(v, carry):
+        fill(v, var_ref.at[v])
+        return carry
+
+    lax.fori_loop(0, p.vars, fill_var, 0)
+    for c, ref in enumerate((east_ref, north_ref, diff_ref)):
+        fill(p.vars + c, ref)
+
+    def wrap(at, carry):
+        wide[at, :, :pad] = wide[at, :, p.lon : p.lon + pad]
+        wide[at, :, pad + p.lon :] = wide[at, :, pad : pad + right]
+        return carry
+
+    lax.fori_loop(0, p.lev * per_level, wrap, 0)
 
     lane = lax.broadcasted_iota(jnp.int32, (1, p.tiles * p.slots), 1)
     filled = jnp.zeros_like(lane)
     for t in range(p.tiles):
-        filled = jnp.where(lane >= t * p.slots, count_ref[0, t], filled)
+        filled = jnp.where(lane >= t * p.slots, jnp.broadcast_to(count_ref[:, t : t + 1], lane.shape), filled)
     weight = jnp.where((lane & (p.slots - 1)) < filled, weight_ref[...], 0.0)
     obs = []
     for x in (weight, weight * value_ref[...], cell_ref[...].astype(jnp.float32)):
@@ -220,9 +242,17 @@
                     piece = jnp.where(lanes >= LANES - borrows, here, piece)
                 out_ref[pl.ds(base + v, p.lat, stride=p.vars), :] = piece
             out_ref[pl.ds(base + p.obs_row, 6), :] = obs
-        return carry
+        leave(z).start()
+        return carry
+
+    def leave(z):
+        count = p.cols * p.rows
+        rows = pl.ds(pl.multiple_of(z * count, 8), count)
+        return pltpu.make_async_copy(out_ref.at[rows, :], out_hbm.at[rows, :], out_sems.at[z])
 
     lax.fori_loop(0, p.lev, blocks, 0)
+    for z in range(p.lev):
+        leave(z).wait()
 
 
 class Stores:
@@ -605,8 +635,9 @@
     looped(p.count, 4, join)
 
 
-def finish_kernel(plan, recv_ref, var_ref, out_ref):
+def finish_kernel(plan, recv_ref, var_hbm, out_ref, wide, var_ref, sems):
     p = plan
+    (copy,) = fetch([var_hbm], [var_ref], sems)
 
     def level(z, carry):
         for j in range(p.cols):
@@ -618,13 +649,22 @@
                 while at < end:
                     i, low = divmod(at, LANES)
                     size = min(end - at, LANES - low)
-                    cols = slice(col, col + size)
-                    scale = -0.5 * var_ref[v, z, :, cols]
-                    out_ref[v, z, :, cols] = scale * rows[i][:, low : low + size]
+                    wide[v, z, :, col : col + size] = rows[i][:, low : low + size]
                     at, col = at + size, col + size
         return carry
 
     lax.fori_loop(0, p.lev, level, 0)
+
+    copy.wait()
+
+    def scale(v, carry):
+        for low in range(0, p.lon, LANES):
+            cols = slice(low, min(low + LANES, p.lon))
+            got = jnp.swapaxes(wide[v, :, :, cols], 0, 1)
+            out_ref[v, :, :, cols] = -0.5 * (var_ref[v, :, :, cols] * got)
+        return carry
+
+    lax.fori_loop(0, p.vars, scale, 0)
 
 
 def transposed(
@@ -634,25 +674,36 @@
     f32 = jnp.float32
     vmem = pl.BlockSpec(memory_space=pltpu.VMEM)
     params = pltpu.CompilerParams(vmem_limit_bytes=VMEM_LIMIT)
-    var = background_var[0]
-    packed = pl.pallas_call(
-        functools.partial(pack_kernel, p),
-        out_shape=jax.ShapeDtypeStruct((p.count * p.rows, LANES), f32),
-        in_specs=[pl.BlockSpec(memory_space=pltpu.SMEM)] + [vmem] * 7,
-        out_specs=vmem,
-        scratch_shapes=[pltpu.VMEM(((p.vars + 3) * p.lev, p.lat, 15 * LANES), f32)],
-        compiler_params=params,
-        name="pack",
-    )(
+
+    def swap(x):
+        return jnp.swapaxes(x, -3, -2)
+
+    var = swap(background_var[0])
+    anywhere = pl.BlockSpec(memory_space=pltpu.HBM)
+    inputs = (
         obs_count.reshape(1, -1),
         obs_cell.reshape(1, -1),
         obs_value.reshape(1, -1),
         obs_weight.reshape(1, -1),
-        advect_east[0],
-        advect_north[0],
-        diffusion[0],
+        swap(advect_east[0]),
+        swap(advect_north[0]),
+        swap(diffusion[0]),
         var,
     )
+    packed = pl.pallas_call(
+        functools.partial(pack_kernel, p),
+        out_shape=jax.ShapeDtypeStruct((p.count * p.rows, LANES), f32),
+        in_specs=[anywhere] * len(inputs),
+        out_specs=anywhere,
+        scratch_shapes=[
+            pltpu.VMEM(((p.vars + 3) * p.lev, p.lat, 15 * LANES), f32),
+            pltpu.VMEM((p.count * p.rows, LANES), f32),
+        ]
+        + [pltpu.VMEM(x.shape, x.dtype) for x in inputs]
+        + [pltpu.SemaphoreType.DMA((len(inputs),)), pltpu.SemaphoreType.DMA((p.lev,))],
+        compiler_params=pltpu.CompilerParams(vmem_limit_bytes=PACK_LIMIT),
+        name="pack",
+    )(*inputs)
     received = lax.all_to_all(packed.reshape(-1, 2, LANES), ("tm", "tile"), 0, 0, tiled=True)
     received = received.reshape(-1, LANES)
     wide = pltpu.VMEM((p.wide * p.pitch, 2 * p.vars, LANES), f32)
@@ -686,12 +737,17 @@
     increment = pl.pallas_call(
         functools.partial(finish_kernel, p),
         out_shape=jax.ShapeDtypeStruct(var.shape, f32),
-        in_specs=[vmem] * 2,
+        in_specs=[vmem, anywhere],
         out_specs=vmem,
+        scratch_shapes=[
+            pltpu.VMEM((p.vars, p.lev, p.lat, p.lon), f32),
+            pltpu.VMEM(var.shape, f32),
+            pltpu.SemaphoreType.DMA((1,)),
+        ],
         compiler_params=params,
         name="finish",
     )(returned, var)
-    return increment[None]
+    return swap(increment)[None]
 
 
 def solution(mesh):

time: 80.9 us -> 81.7 us (level)
  Pallas kernels: 13.4 us -> 17.5 us
  local copies, waits for them, and re-layouts: 3.53 us -> 0.01 us
    pallas_call x1, Pallas kernels: 1.94 us -> 4.77 us  [transposed(): pl.pallas_call(functools.partial(pack_kernel, p), out_shape=jax.ShapeDtyp...]
    unnamed x14 -> x2, local copies, waits for them, and re-layouts: 2.2 us -> 0.01 us
    pallas_call x1, Pallas kernels: 0.52 us -> 1.79 us  [transposed(): pl.pallas_call(functools.partial(finish_kernel, p), out_shape=jax.ShapeDt...]
    broadcast_in_dim x1 -> x0, local copies, waits for them, and re-layouts: 1.27 us -> none  [transposed(): return increment[None]]
where the time goes in v3:
time: 81.7 us; the launch traced here: 81.4 us
  blocking collectives  63.9 us (78%)
  Pallas kernels  17.5 us (21%)
    all_to_all x1, blocking collectives, transposed(): lax.all_to_all(packed.reshape(-1, 2, LANES), ('tm', 'tile'), 0, 0, tiled=...  44 us
    all_to_all x1, blocking collectives, transposed(): returned = lax.all_to_all(back, ('tm', 'tile'), 0, 0, tiled=True)  19.8 us
    pallas_call x1, Pallas kernels, transposed(): pl.pallas_call(functools.partial(chain_kernel, p), out_shape=jax.ShapeDty...  11 us
    pallas_call x1, Pallas kernels, transposed(): pl.pallas_call(functools.partial(pack_kernel, p), out_shape=jax.ShapeDtyp...  4.77 us
    pallas_call x1, Pallas kernels, transposed(): pl.pallas_call(functools.partial(finish_kernel, p), out_shape=jax.ShapeDt...  1.79 us

profile of v3, /device:TPU:0, one launch (start us, length us, event | category | flops | bytes accessed | tf_op | source)
XLA Modules:
  0.0 81.4 jit_solution(8452931425427808910)
XLA Ops:
  0.0 4.8 %pack.1 = f32[2880,128]{1,0:T(8,128)} custom-call(s32[1,8]{1,0:T(1,128)} %bitcast.35, s32[1,256]{1,0:T(1,128)} %bitcast.32, f32[1,256]{1,0:T(1,128)} %bitcast.33, f32[1,256]{1,0:T(1,128)} %bitcast.34, f32[12,2,1440]{2,1,0:T(2,128)} %bitcast.29, f32[12,2,1440]{2,1,0:T(2,128)} %bitcast.30, f32[12,2,1440]{2,1,0:T(2,128)} %bitcast.31, f32[4,12,2,1440]{3,2,1,0:T(2,128)} %bitcast.25), custom_call_target="tpu_custom_call" | custom-call | tf_op jit(solution)/shard_map/pack/pallas_call | solution.py:693
  4.8 44.0 %all_to_all.10 = f32[1440,2,128]{2,1,0:T(2,128)S(1)} all-to-all(f32[1440,2,128]{2,1,0:T(2,128)} %bitcast.28), channel_id=1, replica_groups=mesh['tm'=4,'tile'=8] {'tm','tile'}, dimensions={0} | all-to-all | bytes 2949120 | tf_op jit(solution)/shard_map/all_to_all | solution.py:707
  48.8 0.0 copy-start
  48.8 11.0 %chains.1 = f32[1152,128]{1,0:T(8,128)S(1)} custom-call(f32[2880,128]{1,0:T(8,128)S(1)} %bitcast.23), custom_call_target="tpu_custom_call" | custom-call | tf_op jit(solution)/shard_map/chains/pallas_call | solution.py:712
  59.8 19.8 %all_to_all.11 = f32[288,4,128]{2,1,0:T(4,128)S(1)} all-to-all(f32[288,4,128]{2,1,0:T(4,128)S(1)} %bitcast.27), channel_id=1, replica_groups=mesh['tm'=4,'tile'=8] {'tm','tile'}, dimensions={0} | all-to-all | bytes 1179648 | tf_op jit(solution)/shard_map/all_to_all | solution.py:735
  79.6 0.0 copy-done
  79.6 1.8 %finish.1 = f32[4,12,2,1440]{3,2,1,0:T(2,128)} custom-call(f32[1152,128]{1,0:T(8,128)S(1)} %bitcast.24, f32[4,12,2,1440]{3,2,1,0:T(2,128)S(1)} %bitcast.26), custom_call_target="tpu_custom_call" | custom-call | tf_op jit(solution)/shard_map/finish/pallas_call | solution.py:737
Async XLA Ops:
  48.8 30.8 %copy-start = (f32[1,4,2,12,1440]{4,2,3,1,0:T(2,128)S(1)}, f32[1,4,2,12,1440]{4,2,3,1,0:T(2,128)}, u32[]{:S(2)}) copy-start(f32[1,4,2,12,1440]{4,2,3,1,0:T(2,128)} %param.11) | copy-start | bytes 1658884

commit v4 on v1

--- a/solution.py
+++ b/solution.py
@@ -363,7 +363,7 @@
             stores.put(obs_tab, (i + 1, rows), two)
             stores.put(obs_tab, (i + 2, rows), x - one - two)
 
-    looped(p.subs, 1, observe)
+    looped(p.subs, 2, observe)
 
     n_rows = p.lat * p.vars
     slots = p.tiles * p.slots
@@ -445,7 +445,7 @@
         double(kt, stores)
         widen(kt, stores)
 
-    looped(p.count, 4, prepare)
+    looped(p.count, 8, prepare)
 
     def wide_step(i, carry):
         k = p.wide - 1 - i // STEPS

time: 81.3 us -> 81.7 us (level)
  no operation moved by 1% of the time
where the time goes in v4:
time: 81.7 us; the launch traced here: 81.5 us
  blocking collectives  63.7 us (78%)
  Pallas kernels  14.2 us (17%)
  local copies, waits for them, and re-layouts  3.53 us (4%)
    all_to_all x1, blocking collectives, transposed(): lax.all_to_all(packed.reshape(-1, 2, LANES), ('tm', 'tile'), 0, 0, tiled=...  43.8 us
    all_to_all x1, blocking collectives, transposed(): returned = lax.all_to_all(back, ('tm', 'tile'), 0, 0, tiled=True)  19.8 us
    pallas_call x1, Pallas kernels, transposed(): pl.pallas_call(functools.partial(chain_kernel, p), out_shape=jax.ShapeDty...  11.7 us
    unnamed x14, local copies, waits for them, and re-layouts  2.2 us
    pallas_call x1, Pallas kernels, transposed(): pl.pallas_call(functools.partial(pack_kernel, p), out_shape=jax.ShapeDtyp...  1.94 us

profile of v4, /device:TPU:0, one launch (start us, length us, event | category | flops | bytes accessed | tf_op | source)
XLA Modules:
  0.0 81.5 jit_solution(3868908957173553796)
XLA Ops:
  0.0 0.0 copy-start.4
  0.0 0.0 copy-start.5
  0.0 0.0 copy-start.3
  0.0 0.0 copy-start.2
  0.0 0.0 copy-start.1
  0.0 0.0 copy-start
  0.0 1.0 %copy.19 = f32[1,2,12,1440]{3,2,1,0:T(8,128)S(1)} copy(f32[1,2,12,1440]{3,1,2,0:T(2,128)} %param.8) | data formatting | bytes 276480 | tf_op args[0]
  1.0 1.2 %copy.18 = f32[1,4,2,12,1440]{4,3,2,1,0:T(8,128)S(1)} copy(f32[1,4,2,12,1440]{4,2,3,1,0:T(2,128)} %param.11) | data formatting | bytes 1105920 | tf_op args[3]
  2.2 0.0 copy-done.4
  2.2 0.0 copy-done.5
  2.2 0.1 copy_bitcast_fusion.1
  2.3 0.0 copy-done.3
  2.3 0.0 copy-done.2
  2.3 0.0 copy-done.1
  2.3 0.0 copy-done
  2.3 1.9 %pack.1 = f32[2880,128]{1,0:T(8,128)S(1)} custom-call(s32[1,8]{1,0:T(1,128)S(1)} %bitcast.30, s32[1,256]{1,0:T(1,128)S(1)} %bitcast.27, f32[1,256]{1,0:T(1,128)S(1)} %bitcast.28, f32[1,256]{1,0:T(1,128)S(1)} %bitcast.29, f32[2,12,1440]{2,1,0:T(8,128)S(1)} %bitcast.26, f32[2,12,1440]{2,1,0:T(8,128)S(1)} %get-tuple-element.6.north_ref, ...), custom_call_target="tpu_custom_call" | custom-call | tf_op jit(solution)/shard_map/pack/pallas_call | solution.py:623
  4.3 43.8 %all_to_all.10 = f32[1440,2,128]{2,1,0:T(2,128)S(1)} all-to-all(f32[1440,2,128]{2,1,0:T(2,128)S(1)} %bitcast.21), channel_id=1, replica_groups=mesh['tm'=4,'tile'=8] {'tm','tile'}, dimensions={0} | all-to-all | bytes 2949120 | tf_op jit(solution)/shard_map/all_to_all | solution.py:641
  48.1 11.7 %chains.1 = f32[1152,128]{1,0:T(8,128)S(1)} custom-call(f32[2880,128]{1,0:T(8,128)S(1)} %bitcast.22), custom_call_target="tpu_custom_call" | custom-call | tf_op jit(solution)/shard_map/chains/pallas_call | solution.py:646
  59.8 19.8 %all_to_all.11 = f32[288,4,128]{2,1,0:T(4,128)S(1)} all-to-all(f32[288,4,128]{2,1,0:T(4,128)S(1)} %bitcast.25), channel_id=1, replica_groups=mesh['tm'=4,'tile'=8] {'tm','tile'}, dimensions={0} | all-to-all | bytes 1179648 | tf_op jit(solution)/shard_map/all_to_all | solution.py:668
  79.7 0.5 finish.1
  80.2 1.3 %copy.13 = f32[1,4,2,12,1440]{4,2,3,1,0:T(2,128)} copy(f32[1,4,2,12,1440]{4,3,2,1,0:T(8,128)S(1)} %bitcast.23) | data formatting | bytes 1105920 | tf_op jit(solution)/shard_map/broadcast_in_dim | solution.py:678
Async XLA Ops:
  0.0 2.2 %copy-start.4 = (f32[1,2,12,1440]{3,1,2,0:T(2,128)S(1)}, f32[1,2,12,1440]{3,1,2,0:T(2,128)}, u32[]{:S(2)}) copy-start(f32[1,2,12,1440]{3,1,2,0:T(2,128)} %param.10) | copy-start | bytes 414724
  0.0 2.2 %copy-start.5 = (f32[1,2,12,1440]{3,1,2,0:T(2,128)S(1)}, f32[1,2,12,1440]{3,1,2,0:T(2,128)}, u32[]{:S(2)}) copy-start(f32[1,2,12,1440]{3,1,2,0:T(2,128)} %param.9) | copy-start | bytes 414724
  0.0 2.3 %copy-start.3 = (s32[1,1,8]{2,1,0:T(1,128)S(1)}, s32[1,1,8]{2,1,0:T(1,128)}, u32[]{:S(2)}) copy-start(s32[1,1,8]{2,1,0:T(1,128)} %param.15) | copy-start | bytes 100
  0.0 2.3 %copy-start.2 = (f32[1,1,256]{2,1,0:T(1,128)S(1)}, f32[1,1,256]{2,1,0:T(1,128)}, u32[]{:S(2)}) copy-start(f32[1,1,256]{2,1,0:T(1,128)} %param.14) | copy-start | bytes 3076
  0.0 2.3 %copy-start.1 = (f32[1,1,256]{2,1,0:T(1,128)S(1)}, f32[1,1,256]{2,1,0:T(1,128)}, u32[]{:S(2)}) copy-start(f32[1,1,256]{2,1,0:T(1,128)} %param.13) | copy-start | bytes 3076
  0.0 2.3 %copy-start = (s32[1,1,256]{2,1,0:T(1,128)S(1)}, s32[1,1,256]{2,1,0:T(1,128)}, u32[]{:S(2)}) copy-start(s32[1,1,256]{2,1,0:T(1,128)} %param.12) | copy-start | bytes 3076
